TPU v7x, 128 devices: a whole 4x4x4 slice. The times are simulated.
128 devices in a mesh: freq: 4 (over z), chan: 32 (over x, y, core).
Axes of the slice: x: 4, y: 4, z: 4, core: 2. Of those that a mesh axis runs over, the one named last changes fastest.
Arguments:
- raw_strain: bfloat16 [32, 32, 150000], P('chan', 'freq'), may hold values from -6 to 6
- fir_taps: bfloat16 [20], replicated, may hold values from -1.25 to 1.25
- band_bins: int32 [240], replicated, may hold values from 60 to 359, as said below
- live_mask: int32 [32, 32], P('chan', 'freq'), may hold values 0 or 1
Outputs:
- cross_spectra: float32 [240, 2, 1024, 1024], P('freq', None, 'chan')
Inputs may be any that keep to these rules, and one draw needn't show every extreme that they name: `band_bins`: strictly increasing; the first is 60 and the last is 359.
All inputs are finite; a program needn't handle non-finite values. No bound on the sum of `live_mask` on one device may be relied on, other than what follows from the above.
Results may differ from a plain program's by a relative error of at most 0.0067.
Values may be sent and summed in bfloat16 or wider, within the bound.
A program may use at most 64 MiB of HBM per device.

v0:
```python
import math

import jax
import jax.numpy as jnp
from jax import lax
from jax.sharding import PartitionSpec as P

WIN = 10
DECIM = 10
NT = 1500


def make_table(band_bins, length):
    times = jnp.arange(length, dtype=jnp.int32)[:, None]
    phase = times * band_bins[None, :] % length
    angle = phase.astype(jnp.float32) * jnp.float32(2.0 * math.pi / length)
    return jnp.concatenate([jnp.cos(angle), -jnp.sin(angle)], axis=1).astype(jnp.bfloat16)


def correlate(rows_spec, cols_spec, windows):
    bins = rows_spec.shape[0]
    height = rows_spec.shape[3]
    width = cols_spec.shape[3]
    real_left = rows_spec.reshape(bins, 2 * windows, height)
    imag_left = jnp.concatenate([rows_spec[:, 1], -rows_spec[:, 0]], axis=1)
    left_both = jnp.stack([real_left, imag_left], axis=1)
    right_side = cols_spec.reshape(bins, 2 * windows, width)
    prod = jnp.einsum("fski,fkj->fsij", left_both, right_side, preferred_element_type=jnp.float32)
    return prod / windows


def decimate(raw_strain, fir_taps, rows, windows, length, factor):
    outputs = length // 10
    span = outputs * factor
    blocks = raw_strain.reshape(rows * windows * 10, span)
    taps_float = fir_taps.astype(jnp.float32)
    tap_count = fir_taps.shape[0]
    sample_idx = jnp.arange(span, dtype=jnp.int32)[:, None]
    out_idx = jnp.arange(outputs, dtype=jnp.int32)[None, :]
    tap_idx = factor * out_idx + factor - 1 - sample_idx
    valid = (tap_idx >= 0) & (tap_idx < tap_count)
    band = jnp.where(valid, taps_float[jnp.clip(tap_idx, 0, tap_count - 1)], 0.0).astype(
        jnp.bfloat16
    )
    current = jnp.dot(blocks, band, preferred_element_type=jnp.float32)
    tail = blocks[:, span - factor :]
    tail_taps = taps_float[2 * factor - 1 - jnp.arange(factor, dtype=jnp.int32)].astype(
        jnp.bfloat16
    )
    carried = jnp.dot(tail, tail_taps[:, None], preferred_element_type=jnp.float32)
    carried = carried.reshape(rows * windows, 10)
    carried = jnp.pad(carried, ((0, 0), (1, 0)))[:, :10]
    current = current.reshape(rows * windows, 10, outputs)
    current = current.at[:, :, 0].add(carried)
    return current.reshape(rows, windows, length).astype(jnp.bfloat16)


def shards(raw_strain, fir_taps, band_bins, live_mask):
    rows = raw_strain.shape[1]
    windows = WIN
    length = NT
    factor = DECIM
    bins = band_bins.shape[0]
    table = make_table(band_bins, length)
    decimated = decimate(raw_strain, fir_taps, rows, windows, length, factor)
    spectrum = jnp.dot(
        decimated.reshape(rows * windows, length), table, preferred_element_type=jnp.float32
    )
    spectrum = spectrum.reshape(rows, windows, 2, bins)
    power = jnp.sum(spectrum * spectrum, axis=(2, 3)) / bins
    scale = lax.rsqrt(power + 1e-06) * live_mask[0].astype(jnp.float32)[:, None]
    whitened = (spectrum * scale[:, :, None, None]).astype(jnp.bfloat16)
    ordered = jnp.transpose(whitened, (3, 2, 1, 0))
    own = lax.all_to_all(ordered, "freq", split_axis=0, concat_axis=3, tiled=True)
    return correlate(own, lax.all_gather(own, "chan", axis=3, tiled=True), windows)


def solution(mesh):
    in_specs = (P("chan", "freq", None), P(), P(), P("chan", "freq"))
    out_specs = P("freq", None, "chan", None)
    return jax.shard_map(shards, mesh=mesh, in_specs=in_specs, out_specs=out_specs, check_vma=False)
```

profile of v0, /device:TPU:1, one launch (start us, length us, event | category | flops | bytes accessed | tf_op | source)
XLA Modules:
  0.0 153.3 jit_solution(7319070149672299700)
XLA Ops:
  6.5 0.0 all-gather.2.cloned.1.call-start
  6.5 1.3 slice.57
  7.9 2.1 %fusion.129 = (bf16[1]{0:T(256)(128)(2,1)}, bf16[1]{0:T(256)(128)(2,1)}, bf16[1]{0:T(256)(128)(2,1)}, bf16[1]{0:T(256)(128)(2,1)}, bf16[1]{0:T(256)(128)(2,1)}, ...) fusion(bf16[20]{0:T(256)(128)(2,1)} %param.7), kind=kLoop, calls=%fused_computation.157 | loop fusion | bytes 76 | tf_op jit(solution)/shard_map/gather | solution.py:42
  9.9 0.7 convert_bitcast_fusion
  10.6 1.3 gather_fusion
  11.9 8.3 %cosine_convert_fusion = (bf16[1500,240]{0,1:T(8,128)(2,1)S(1)}, bf16[1500,240]{0,1:T(8,128)(2,1)}) fusion(s32[240]{0:T(256)} %param.8), kind=kLoop, calls=%fused_computation.59 | loop fusion | flops 4320000 | bytes 1440960 | tf_op jit(solution)/shard_map/convert
  20.2 4.8 %reshape.254 = bf16[1200000]{0:T(1024)(128)(2,1)S(1)} reshape(bf16[1,8,150000]{2,1,0:T(8,128)(2,1)} %param.6) | data formatting | bytes 4800000
  25.0 5.0 %reshape.153 = bf16[800,1500]{1,0:T(8,128)(2,1)} reshape(bf16[1200000]{0:T(1024)(128)(2,1)S(1)} %reshape.254) | data formatting | bytes 4800000 | tf_op jit(solution)/shard_map/reshape | solution.py:35
  30.0 1.0 slice.63
  31.0 0.1 copy.52
  31.2 0.2 dot_general.24
  31.4 0.1 multiply_reduce_fusion
  31.5 0.1 copy.44
  31.6 17.4 %convolution_bitcast_fusion = f32[800,150]{0,1:T(8,128)S(1)} fusion(bf16[800,1500]{1,0:T(8,128)(2,1)} %reshape.153, bf16[]{:T(256)} %bitcast.27, bf16[]{:T(256)} %bitcast.28, bf16[]{:T(256)} %bitcast.29, bf16[]{:T(256)} %bitcast.30, bf16[]{:T(256)} %bitcast.31, bf16[]{:T(256)} %bitcast.33, bf16[]{:T(256)} %bitcast.32, bf16[]{:T(256)} %bitcast.2, ...), kind=kOutput, calls=%fused_computation.64 | convolution fusion | flops 370800000 | bytes 2880640 | tf_op jit(solution)/shard_map/dot_general | solution.py:45
  49.0 0.3 copy.30
  49.3 0.1 reshape.154
  49.4 1.2 copy.32
  50.6 1.2 slice_add_fusion
  51.8 5.3 %scatter-add.4 = f32[80,10,150]{2,1,0:T(8,128)S(1)} dynamic-update-slice(f32[80,10,150]{2,1,0:T(8,128)S(1)} %reshape.154, f32[80,10,1]{2,1,0:T(8,128)S(1)} %slice_add_fusion, s32[]{:T(128)} %constant.58.clone.1, s32[]{:T(128)} %constant.58.clone.1, s32[]{:T(128)} %constant.58.clone.1) | dynamic-update-slice | bytes 6404 | tf_op jit(solution)/shard_map/scatter-add | solution.py:54
  57.1 0.0 copy-start
  57.1 0.9 convert_element_type.42
  58.0 1.8 %reshape.250 = bf16[8,10,1500,1]{2,1,0,3:T(8,128)(2,1)S(1)} reshape(bf16[80,10,150]{2,1,0:T(8,128)(2,1)} %convert_element_type.42) | data formatting | bytes 480000 | tf_op jit(solution)/shard_map/convert_element_type | solution.py:55
  59.8 0.0 copy-done
  59.8 0.1 pad_maximum_fusion
  59.9 0.7 multiply_reduce_fusion.1
  60.6 0.1 multiply_bitcast_fusion
  60.7 0.1 fusion.103
  60.8 1.4 copy.33
  62.2 1.6 %reshape.256 = bf16[4,2,4800]{2,1,0:T(2,128)(2,1)S(1)} reshape(bf16[240,8,2,10]{3,2,1,0:T(2,128)(2,1)S(1)} %bitcast.166) | data formatting | bytes 153600
  63.8 10.2 %all_to_all.18 = bf16[4,2,4800]{2,1,0:T(2,128)(2,1)S(1)} all-to-all(bf16[4,2,4800]{2,1,0:T(2,128)(2,1)S(1)} %reshape.256), channel_id=1, replica_groups=mesh['freq'=4,'chan'=32] {'freq'}, dimensions={0} | all-to-all | bytes 153600 | tf_op jit(solution)/shard_map/all_to_all | solution.py:74
  74.0 2.3 %reshape.257 = bf16[240,8,2,10]{3,2,1,0:T(2,128)(2,1)S(1)} reshape(bf16[4,2,4800]{2,1,0:T(2,128)(2,1)S(1)} %all_to_all.18) | data formatting | bytes 153600
  76.3 1.3 copy.47
  77.6 0.7 copy.55
  78.3 0.0 all-gather.2.cloned.1.call-update
  78.4 0.9 slice_bitcast_fusion
  79.4 1.0 pad_maximum_fusion.1
  80.4 1.5 copy.38
  81.8 49.7 %all-gather.2.cloned.1.call-done = bf16[60,2,10,1024]{0,3,2,1:T(8,128)(2,1)} async-done(((bf16[60,2,10,32]{0,3,2,1:T(8,128)(2,1)}), bf16[60,2,10,1024]{0,3,2,1:T(8,128)(2,1)}) %all-gather.2.cloned.1.call-update) | async-done | bytes 2457616 | tf_op jit(solution)/shard_map/all_gather | solution.py:75
  131.5 6.8 %copy.46 = bf16[60,20,1024,1]{2,1,3,0:T(8,128)(2,1)S(1)} copy(bf16[60,20,1024,1]{0,2,1,3:T(8,128)(2,1)} %bitcast.165) | data formatting | bytes 4915200 | tf_op jit(solution)/shard_map/reshape | solution.py:27
  138.3 8.2 %convolution_multiply_fusion = f32[60,2,32,1024]{3,2,1,0:T(8,128)} fusion(bf16[60,2,20,32]{3,2,1,0:T(8,128)(2,1)} %copy.38, bf16[60,20,1024,1]{2,1,3,0:T(8,128)(2,1)S(1)} %copy.46), kind=kOutput, calls=%fused_computation.1 | convolution fusion | flops 161218560 | bytes 18339840 | tf_op jit(solution)/shard_map/fski,fkj->fsij/dot_general | solution.py:28
  (6 shorter events, 0.1 us)
Async XLA Ops:
  6.5 125.0 %all-gather.2.cloned.1.call-start = ((), (), s32[]{:S(2)}) async-start(), calls=%async_computation.1 | async-start | bytes 5406720 | tf_op jit(solution)/shard_map/all_gather | solution.py:75
  57.1 2.7 %copy-start = (bf16[1500,240]{0,1:T(8,128)(2,1)S(1)}, bf16[1500,240]{0,1:T(8,128)(2,1)}, u32[]{:S(2)}) copy-start(bf16[1500,240]{0,1:T(8,128)(2,1)} %get-tuple-element.22) | copy-start | bytes 2160004
Sparse Core Ops, SparseCore 0:
  78.5 52.9 all-gather.1
where the time goes:
time: 154 us; the launch traced here: 153 us
  waiting for transfers between devices  49.7 us (32%)
  local copies, waits for them, and re-layouts  40.1 us (26%)
  matrix products  26.3 us (17%)
  between operations  13.6 us (9%)
  other arithmetic  13.5 us (9%)
  blocking collectives  10.2 us (7%)
    all_gather x1, waiting for transfers between devices, shards(): lax.all_gather(own, 'chan', axis=3, tiled=True)  49.7 us
    dot_general x1, matrix products, decimate(): current = jnp.dot(blocks, band, preferred_element_type=jnp.float32)  17.4 us
    all_to_all x1, blocking collectives, shards(): lax.all_to_all(ordered, 'freq', split_axis=0, concat_axis=3, tiled=True)  10.2 us
    unnamed x6, local copies, waits for them, and re-layouts  8.8 us
    another operation x1, other arithmetic  8.32 us
    dot_general x1, matrix products, correlate(): jnp.einsum('fski,fkj->fsij', left_both, right_side, preferred_element_typ...  8.19 us
    reshape x1, local copies, waits for them, and re-layouts, correlate(): right_side = cols_spec.reshape(bins, 2 * windows, width)  6.79 us
    scatter-add x1, local copies, waits for them, and re-layouts, decimate(): current = current.at[:, :, 0].add(carried)  5.28 us
  transfers between devices with their start and end apart: 1, of which 1 were waited for; matrix products, arithmetic and copies ran while one was open for 2% of the time, Pallas kernels for 0%

commit v1 on v0

v1 whole, which is shorter than its diff:
```python
import functools
import math

import jax
import jax.numpy as jnp
from jax import lax
from jax.experimental import pallas as pl
from jax.experimental.pallas import tpu as pltpu
from jax.sharding import PartitionSpec as P

WIN = 10
DECIM = 10
NT = 1500
TAPS = 20
BINS = 240
ROWS = 8
TILE = 128
SPAN = TILE * DECIM
SAMPLES = WIN * NT * DECIM
TILES = -(-SAMPLES // SPAN)
NTP = 12 * TILE
GROUP = 12
PACK = 5 * TILE
WIDE = 5 * 256
F32 = jnp.float32
BF16 = jnp.bfloat16
I32 = jnp.int32
MESH = pl.DeviceIdType.MESH


def iota(shape, axis):
    return lax.broadcasted_iota(I32, shape, axis)


def build_fir(taps_ref, fir_ref):
    row = iota((80, TAPS), 0)
    phase = row % DECIM
    tap = iota((80, TAPS), 1)
    taps = jnp.broadcast_to(taps_ref[...].astype(F32), (80, TAPS))
    near = jnp.sum(jnp.where(tap == 9 - phase, taps, 0.0), axis=1, keepdims=True)
    far = jnp.sum(jnp.where(tap == 19 - phase, taps, 0.0), axis=1, keepdims=True)
    near = jnp.broadcast_to(near, (80, 256))
    far = jnp.broadcast_to(far, (80, 256))
    gap = iota((80, 256), 1) - iota((80, 256), 0) // DECIM
    for step in range(SPAN // 80):
        block = jnp.where(gap == 8 * step, near, jnp.where(gap == 8 * step + 1, far, 0.0))
        fir_ref[80 * step : 80 * step + 80, :] = block.astype(BF16)


def build_table(bins_ref, table_ref):
    bins = bins_ref[...].astype(F32)
    bins = jnp.concatenate([bins, jnp.zeros((1, 16), F32)], axis=1)
    row = iota((40, 256), 0)
    times = jnp.where(row < 8, row, jnp.where(row < 24, 8 * (row - 8), 128 * (row - 24)))
    product = times.astype(F32) * bins
    turns = jnp.floor(product * (1.0 / NT))
    left = product - turns * NT
    left = jnp.where(left < 0, left + NT, left)
    left = jnp.where(left >= NT, left - NT, left)
    angle = left * F32(2.0 * math.pi / NT)
    re = jnp.cos(angle)
    im = -jnp.sin(angle)
    kept = iota((40, 256), 1) < BINS
    re = jnp.where(kept, re, 0.0)
    im = jnp.where(kept, im, 0.0)
    base_re, base_im = [], []
    for b in range(16):
        tr, ti = re[8 + b : 9 + b], im[8 + b : 9 + b]
        base_re.append(re[0:8] * tr - im[0:8] * ti)
        base_im.append(re[0:8] * ti + im[0:8] * tr)
    base_re = jnp.concatenate(base_re, axis=0)
    base_im = jnp.concatenate(base_im, axis=0)
    for a in range(12):
        tr, ti = re[24 + a : 25 + a], im[24 + a : 25 + a]
        block_re = base_re * tr - base_im * ti
        block_im = base_re * ti + base_im * tr
        if a == 11:
            inside = iota((TILE, 256), 0) < NT - 11 * TILE
            block_re = jnp.where(inside, block_re, 0.0)
            block_im = jnp.where(inside, block_im, 0.0)
        table_ref[TILE * a : TILE * a + TILE, 0:256] = block_re.astype(BF16)
        table_ref[TILE * a : TILE * a + TILE, 256:512] = block_im.astype(BF16)


def build_left(x_ref, left_ref):
    def tile(t):
        return x_ref[0, :, SPAN * t : min(SPAN * t + SPAN, SAMPLES)].astype(F32)

    blocks = []
    for t in range(TILES):
        blocks.append((t, None))
    for w in range(1, WIN):
        t = NT * w // TILE
        blocks.append((t, NT * DECIM * w - SPAN * t))
    blocks.append((None, None))

    def value(block):
        t, first = block
        if t is None:
            return jnp.zeros((ROWS, SPAN), F32)
        part = tile(t)
        if part.shape[1] < SPAN:
            part = jnp.concatenate([part, jnp.zeros((ROWS, SPAN - part.shape[1]), F32)], axis=1)
        if first is not None:
            part = jnp.where(iota((ROWS, SPAN), 1) < first, 0.0, part)
        return part

    for pair in range(len(blocks) // 2):
        both = jnp.concatenate([value(blocks[2 * pair]), value(blocks[2 * pair + 1])], axis=0)
        left_ref[16 * pair : 16 * pair + 16, :] = both.astype(BF16)


def align_windows(res_ref, dec_ref):
    lane = iota((ROWS, TILE), 1)

    def plain(t):
        main = res_ref[8 * t : 8 * t + 8, 0:TILE]
        if t == 0:
            return main
        return main + res_ref[8 * t - 8 : 8 * t, TILE : 2 * TILE]

    def window(w):
        t = NT * w // TILE
        shift = NT * w - TILE * t
        tiles = [plain(t + u) for u in range(1, 13 if shift else 12)]
        if w == 0:
            first = plain(0)
        else:
            at = 8 * (TILES + w - 1)
            first = res_ref[at : at + 8, 0:TILE]
        tiles = [first] + tiles
        if shift:
            rolled = [pltpu.roll(one, TILE - shift, 1) for one in tiles]
            tiles = [
                jnp.where(lane < TILE - shift, rolled[u], rolled[u + 1]) for u in range(12)
            ]
        return jnp.concatenate(tiles, axis=1)

    for pair in range(WIN // 2):
        both = jnp.concatenate([window(2 * pair), window(2 * pair + 1)], axis=0)
        dec_ref[16 * pair : 16 * pair + 16, :] = both.astype(BF16)


def pack(white, send_ref):
    lane = iota((ROWS, 256), 1)
    segment = lane // GROUP
    wrapped = (lane + 256) // GROUP
    turned = []
    for part in range(2):
        for w in range(WIN):
            spot = part * WIN + w
            piece = white[8 * w : 8 * w + 8, 256 * part : 256 * part + 256]
            turned.append(pltpu.roll(piece, GROUP * spot, 1) if spot else piece)
    for group in range(BINS // GROUP):
        halves = []
        for half in range(2):
            lanes = slice(TILE * half, TILE * half + TILE)
            total = jnp.zeros((ROWS, TILE), F32)
            for spot in range(2 * WIN):
                start = GROUP * (spot + group)
                covers = [
                    at
                    for at in (start, start - 256)
                    if at < TILE * half + TILE and at + GROUP > TILE * half
                ]
                for at in covers:
                    ids = segment if at == start else wrapped
                    total = jnp.where(
                        ids[:, lanes] == spot + group, turned[spot][:, lanes], total
                    )
            halves.append(total)
        dest = jnp.concatenate(halves, axis=1)
        if group:
            dest = pltpu.roll(dest, 256 - GROUP * group, 1)
        both = jnp.concatenate([dest[:, 0:TILE], dest[:, TILE:256]], axis=0)
        z, g = group // 5, group % 5
        send_ref[z, :, TILE * g : TILE * g + TILE] = both.astype(BF16)


def spectra_kernel(x_ref, taps_ref, bins_ref, mask_ref, send_ref, fir_ref, table_ref, left_ref, res_ref, dec_ref):
    build_fir(taps_ref, fir_ref)
    build_table(bins_ref, table_ref)
    build_left(x_ref, left_ref)
    res_ref[...] = jnp.dot(left_ref[...], fir_ref[...], preferred_element_type=F32)
    align_windows(res_ref, dec_ref)
    spectrum = jnp.dot(dec_ref[...], table_ref[...], preferred_element_type=F32)
    power = jnp.sum(spectrum * spectrum, axis=1, keepdims=True) / BINS
    channel = iota((80, 8), 0) % ROWS
    live = jnp.broadcast_to(mask_ref[...].astype(F32), (80, 8))
    live = jnp.sum(jnp.where(channel == iota((80, 8), 1), live, 0.0), axis=1, keepdims=True)
    white = spectrum * (lax.rsqrt(power + 1e-06) * live)
    pack(white, send_ref)


def spectra(raw_strain, fir_taps, band_bins, live_mask):
    vmem = pl.BlockSpec(memory_space=pltpu.VMEM)
    return pl.pallas_call(
        spectra_kernel,
        out_shape=jax.ShapeDtypeStruct((4, 16, PACK), BF16),
        in_specs=[vmem] * 4,
        out_specs=vmem,
        scratch_shapes=[
            pltpu.VMEM((SPAN, 256), BF16),
            pltpu.VMEM((NTP, 512), BF16),
            pltpu.VMEM((1024, SPAN), BF16),
            pltpu.VMEM((1024, 256), F32),
            pltpu.VMEM((80, NTP), BF16),
        ],
        compiler_params=pltpu.CompilerParams(vmem_limit_bytes=32 * 1024 * 1024),
        name="spectra",
    )(raw_strain, fir_taps.reshape(1, TAPS), band_bins.reshape(1, BINS), live_mask)


def gather_kernel(send_ref, own_ref, all_ref, raw, hold, z_send, z_recv, g_send, g_recv, local_sem):
    z = lax.axis_index("freq")
    b = lax.axis_index("chan")
    x, y, c = b // 8, (b // 2) % 4, b % 2

    def index(xx, yy, cc):
        return (xx % 4 * 4 + yy % 4) * 2 + cc

    sibling = index(x, y, 1 - c)
    peers = [((z + d) % 4, b) for d in (1, 2, 3)]
    peers += [(z, index(x + d, y, c)) for d in (1, 3)]
    peers += [(z, index(x, y + d, c)) for d in (1, 3)]
    peers += [(z, sibling)]
    barrier = pltpu.get_barrier_semaphore()
    for peer in peers:
        pl.semaphore_signal(barrier, inc=1, device_id=peer, device_id_type=MESH)
    pl.semaphore_wait(barrier, len(peers))

    crossing = []
    for d in (1, 2, 3):
        to = (z + d) % 4
        copy = pltpu.make_async_remote_copy(
            src_ref=send_ref.at[to], dst_ref=raw.at[z],
            send_sem=z_send.at[d - 1], recv_sem=z_recv.at[d - 1],
            device_id=(to, b), device_id_type=MESH,
        )
        copy.start()
        crossing.append(copy)
    raw[z] = send_ref[z]
    for copy in crossing:
        copy.wait_recv()
    for pair in range(2):
        even = raw[2 * pair].astype(F32)
        odd = raw[2 * pair + 1].astype(F32)
        low = jnp.concatenate([even[0:8], odd[0:8]], axis=0).astype(BF16)
        high = jnp.concatenate([even[8:16], odd[8:16]], axis=0).astype(BF16)
        for g in range(5):
            hold[16 * pair : 16 * pair + 16, 256 * g : 256 * g + TILE] = low[:, TILE * g : TILE * g + TILE]
            hold[16 * pair : 16 * pair + 16, 256 * g + TILE : 256 * g + 256] = high[:, TILE * g : TILE * g + TILE]

    own_copy = pltpu.make_async_copy(hold, own_ref, local_sem.at[0])
    own_copy.start()
    own_all = pltpu.make_async_copy(hold, all_ref.at[b], local_sem.at[1])
    own_all.start()

    started = []
    full, first, second = (0, WIDE), (0, WIDE // 2), (WIDE // 2, WIDE // 2)

    def spot(source, half, lanes):
        return all_ref.at[source, pl.ds(16 * half, 16), pl.ds(*lanes)]

    def push(source, half, lanes, target, held=False):
        at = len(started)
        src = hold.at[pl.ds(16 * half, 16), pl.ds(*lanes)] if held else spot(source, half, lanes)
        copy = pltpu.make_async_remote_copy(
            src_ref=src, dst_ref=spot(source, half, lanes),
            send_sem=g_send.at[at], recv_sem=g_recv.at[at],
            device_id=(z, target), device_id_type=MESH,
        )
        copy.start()
        started.append(copy)
        return copy

    def arrived(copy, source, half, lanes):
        copy.wait_recv()

    def near(half, d):
        return index(x + d, y, c) if half == 0 else index(x, y + d, c)

    def far(half, d):
        return index(x, y + d, c) if half == 0 else index(x + d, y, c)

    def block(half, u, v, cc):
        return index(x + u, y + v, cc) if half == 0 else index(x + v, y + u, cc)

    siblings = []

    def share(half, u, v, held=False):
        copy = push(block(half, u, v, c), half, full, sibling, held)
        siblings.append((copy, half, u, v))

    outer = {}

    def spread(half, u, held=False):
        for d in (1, -1):
            outer[half, u, d] = push(block(half, u, 0, c), half, full, far(half, d), held)

    one = {}
    for half in (0, 1):
        for d in (1, -1):
            one[half, d] = push(b, half, full, near(half, d), True)
    for half in (0, 1):
        spread(half, 0, True)
        share(half, 0, 0, True)
    relay = {}
    for half in (0, 1):
        for d in (1, -1):
            source = block(half, -d, 0, c)
            arrived(one[half, d], source, half, full)
            relay[half, d] = push(source, half, first if d == 1 else second, near(half, d))
    for half in (0, 1):
        for d in (1, -1):
            spread(half, -d)
            share(half, -d, 0)
    onward = {}

    def pass_on(half, u):
        for d in (1, -1):
            source = block(half, u, -d, c)
            arrived(outer[half, u, d], source, half, full)
            onward[half, u, d] = push(source, half, first if d == 1 else second, far(half, d))
            share(half, u, -d)

    def finish(half, u):
        source = block(half, u, 2, c)
        arrived(onward[half, u, 1], source, half, first)
        arrived(onward[half, u, -1], source, half, second)
        share(half, u, 2)

    for half in (0, 1):
        source = block(half, 2, 0, c)
        arrived(relay[half, 1], source, half, first)
        arrived(relay[half, -1], source, half, second)
        spread(half, 2)
        share(half, 2, 0)
    for u in (0, -1, 1, 2):
        for half in (0, 1):
            pass_on(half, u)
    for u in (0, -1, 1, 2):
        for half in (0, 1):
            finish(half, u)
    for copy, half, u, v in siblings:
        arrived(copy, block(half, u, v, 1 - c), half, full)
    for copy in started:
        copy.wait_send()
    for copy in crossing:
        copy.wait_send()
    own_copy.wait()
    own_all.wait()


def gather(send):
    vmem = pl.BlockSpec(memory_space=pltpu.VMEM)
    hbm = pl.BlockSpec(memory_space=pl.ANY)
    count = 72
    return pl.pallas_call(
        gather_kernel,
        out_shape=(
            jax.ShapeDtypeStruct((32, WIDE), BF16),
            jax.ShapeDtypeStruct((32, 32, WIDE), BF16),
        ),
        in_specs=[vmem],
        out_specs=(hbm, hbm),
        scratch_shapes=[
            pltpu.VMEM((4, 16, PACK), BF16),
            pltpu.VMEM((32, WIDE), BF16),
            pltpu.SemaphoreType.DMA((3,)),
            pltpu.SemaphoreType.DMA((3,)),
            pltpu.SemaphoreType.DMA((count,)),
            pltpu.SemaphoreType.DMA((count,)),
            pltpu.SemaphoreType.DMA((2,)),
        ],
        compiler_params=pltpu.CompilerParams(
            collective_id=0, has_side_effects=True, vmem_limit_bytes=8 * 1024 * 1024
        ),
        name="gather",
    )(send)


PER_STEP = 4


def correlate_kernel(own_ref, all_ref, out_ref):
    step = pl.program_id(0) % (GROUP // PER_STEP)
    own = own_ref[...].astype(F32)
    lane = iota((32, 256), 1)
    turned = jnp.where(
        lane < 120, pltpu.roll(own, 256 - 120, 1), jnp.where(lane < 240, -pltpu.roll(own, 120, 1), 0.0)
    )
    bin_of = lane % GROUP
    rows = []
    for f in range(PER_STEP):
        keep = bin_of == step * PER_STEP + f
        rows.append(jnp.where(keep, own, 0.0))
        rows.append(jnp.where(keep, turned, 0.0))
    left = jnp.concatenate(rows, axis=0).astype(BF16)
    right = all_ref[...].reshape(1024, 256)
    prod = lax.dot_general(left, right, (((1,), (1,)), ((), ())), preferred_element_type=F32)
    out_ref[...] = (prod * (1.0 / WIN)).reshape(PER_STEP, 2, 32, 1024)


def correlate(own, everyone):
    per_group = GROUP // PER_STEP
    return pl.pallas_call(
        correlate_kernel,
        out_shape=jax.ShapeDtypeStruct((60, 2, 32, 1024), F32),
        grid=(60 // PER_STEP,),
        in_specs=[
            pl.BlockSpec((32, 256), lambda i: (0, i // per_group)),
            pl.BlockSpec((32, 32, 256), lambda i: (0, 0, i // per_group)),
        ],
        out_specs=pl.BlockSpec((PER_STEP, 2, 32, 1024), lambda i: (i, 0, 0, 0)),
        compiler_params=pltpu.CompilerParams(vmem_limit_bytes=32 * 1024 * 1024),
        name="correlate",
    )(own, everyone)


def shards(raw_strain, fir_taps, band_bins, live_mask):
    send = spectra(raw_strain, fir_taps, band_bins, live_mask)
    own, everyone = gather(send)
    return correlate(own, everyone)


def solution(mesh):
    in_specs = (P("chan", "freq", None), P(), P(), P("chan", "freq"))
    out_specs = P("freq", None, "chan", None)
    return jax.shard_map(shards, mesh=mesh, in_specs=in_specs, out_specs=out_specs, check_vma=False)
```

time: 154 us -> 45.1 us (0.29)
  waiting for transfers between devices: 49.7 us -> 0 us
  Pallas kernels: 0 us -> 41.2 us
  local copies, waits for them, and re-layouts: 40.1 us -> 3.66 us
  matrix products: 26.3 us -> 0 us
  between operations: 13.6 us -> 0.01 us
  other arithmetic: 13.5 us -> 0 us
  blocking collectives: 10.2 us -> 0 us
    all_gather x1 -> x0, waiting for transfers between devices: 49.7 us -> none  [shards(): lax.all_gather(own, 'chan', axis=3, tiled=True)]
    pallas_call x0 -> x3, Pallas kernels: none -> 41.2 us  [the longest x1 28.4 us: gather(): pl.pallas_call(gather_kernel, out_shape=(jax.ShapeDtypeStruct((32, WIDE),...]
    dot_general x3 -> x0, matrix products: 26.3 us -> none  [the longest x1 17.4 us: decimate(): current = jnp.dot(blocks, band, preferred_element_type=jnp.float32)]
    reshape x3 -> x0, local copies, waits for them, and re-layouts: 11.9 us -> none  [the longest x1 6.79 us: correlate(): right_side = cols_spec.reshape(bins, 2 * windows, width)]
    all_to_all x1 -> x0, blocking collectives: 10.2 us -> none  [shards(): lax.all_to_all(ordered, 'freq', split_axis=0, concat_axis=3, tiled=True)]
    another operation x3 -> x0, other arithmetic: 9.35 us -> none
    scatter-add x1 -> x0, local copies, waits for them, and re-layouts: 5.28 us -> none  [decimate(): current = current.at[:, :, 0].add(carried)]
    unnamed x6 -> x8, local copies, waits for them, and re-layouts: 8.8 us -> 3.66 us
  transfers between devices with their start and end apart: 1 -> 0, of which waited for: 1 -> 0; matrix products, arithmetic and copies ran while one was open for 2% -> 0% of each run, Pallas kernels for 0% -> 0%
where the time goes in v1:
time: 45.1 us; the launch traced here: 44.9 us
  Pallas kernels  41.2 us (91%)
  local copies, waits for them, and re-layouts  3.66 us (8%)
    pallas_call x1, Pallas kernels, gather(): pl.pallas_call(gather_kernel, out_shape=(jax.ShapeDtypeStruct((32, WIDE),...  28.4 us
    pallas_call x1, Pallas kernels, correlate(): pl.pallas_call(correlate_kernel, out_shape=jax.ShapeDtypeStruct((60, 2, 3...  10.7 us
    unnamed x8, local copies, waits for them, and re-layouts  3.66 us
    pallas_call x1, Pallas kernels, spectra(): pl.pallas_call(spectra_kernel, out_shape=jax.ShapeDtypeStruct((4, 16, PAC...  2.14 us

profile of v1, /device:TPU:1, one launch (start us, length us, event | category | flops | bytes accessed | tf_op | source)
XLA Modules:
  0.0 44.9 jit_solution(3996787749767652567)
XLA Ops:
  0.0 0.0 copy-start
  0.0 1.7 %copy-done = bf16[1,8,150000]{2,1,0:T(8,128)(2,1)S(1)} copy-done((bf16[1,8,150000]{2,1,0:T(8,128)(2,1)S(1)}, bf16[1,8,150000]{2,1,0:T(8,128)(2,1)}, u32[]{:S(2)}) %copy-start) | copy-done | bytes 2400024
  1.7 0.0 copy-start.1
  1.7 0.7 %copy-done.1 = s32[240]{0:T(256)S(1)} copy-done((s32[240]{0:T(256)S(1)}, s32[240]{0:T(256)}, u32[]{:S(2)}) %copy-start.1) | copy-done | bytes 984
  2.4 0.0 copy-start.2
  2.4 0.7 %copy-done.2 = bf16[20]{0:T(256)(128)(2,1)S(1)} copy-done((bf16[20]{0:T(256)(128)(2,1)S(1)}, bf16[20]{0:T(256)(128)(2,1)}, u32[]{:S(2)}) %copy-start.2) | copy-done | bytes 64
  3.0 0.0 copy-start.3
  3.0 0.7 %copy-done.3 = s32[1,8]{1,0:T(1,128)S(1)} copy-done((s32[1,8]{1,0:T(1,128)S(1)}, s32[1,8]{1,0:T(1,128)}, u32[]{:S(2)}) %copy-start.3) | copy-done | bytes 56
  3.7 2.1 %spectra.1.send_ref = bf16[4,16,640]{2,1,0:T(8,128)(2,1)S(1)} custom-call(bf16[1,8,150000]{2,1,0:T(8,128)(2,1)S(1)} %copy-done, bf16[1,20]{1,0:T(2,128)(2,1)S(1)} %bitcast.3, s32[1,240]{1,0:T(1,128)S(1)} %bitcast.2, s32[1,8]{1,0:T(1,128)S(1)} %copy-done.3), custom_call_target="tpu_custom_call" | custom-call | tf_op jit(solution)/shard_map/spectra/pallas_call | solution.py:197
  5.8 28.4 %gather.1 = (bf16[32,1280]{1,0:T(8,128)(2,1)S(1)}, bf16[32,32,1280]{2,1,0:T(8,128)(2,1)S(1)}) custom-call(bf16[4,16,640]{2,1,0:T(8,128)(2,1)S(1)} %spectra.1.send_ref), custom_call_target="tpu_custom_call" | custom-call | tf_op jit(solution)/shard_map/gather/pallas_call | solution.py:359
  34.2 10.7 %correlate.1 = f32[60,2,32,1024]{3,2,1,0:T(8,128)} custom-call(bf16[32,1280]{1,0:T(8,128)(2,1)S(1)} %get-tuple-element.7.own_ref, bf16[32,32,1280]{2,1,0:T(8,128)(2,1)S(1)} %get-tuple-element.8.all_ref), custom_call_target="tpu_custom_call" | custom-call | tf_op jit(solution)/shard_map/correlate/pallas_call | solution.py:407
Async XLA Ops:
  0.0 1.7 %copy-start = (bf16[1,8,150000]{2,1,0:T(8,128)(2,1)S(1)}, bf16[1,8,150000]{2,1,0:T(8,128)(2,1)}, u32[]{:S(2)}) copy-start(bf16[1,8,150000]{2,1,0:T(8,128)(2,1)} %x_ref.1) | copy-start | bytes 7200004
  1.7 0.7 %copy-start.1 = (s32[240]{0:T(256)S(1)}, s32[240]{0:T(256)}, u32[]{:S(2)}) copy-start(s32[240]{0:T(256)} %param.6) | copy-start | bytes 2884
  2.4 0.7 %copy-start.2 = (bf16[20]{0:T(256)(128)(2,1)S(1)}, bf16[20]{0:T(256)(128)(2,1)}, u32[]{:S(2)}) copy-start(bf16[20]{0:T(256)(128)(2,1)} %param.5) | copy-start | bytes 124
  3.0 0.7 %copy-start.3 = (s32[1,8]{1,0:T(1,128)S(1)}, s32[1,8]{1,0:T(1,128)}, u32[]{:S(2)}) copy-start(s32[1,8]{1,0:T(1,128)} %mask_ref.1) | copy-start | bytes 100

commit v2 on v1

--- a/solution.py
+++ b/solution.py
@@ -86,9 +86,7 @@
     def tile(t):
         return x_ref[0, :, SPAN * t : min(SPAN * t + SPAN, SAMPLES)].astype(F32)
 
-    blocks = []
-    for t in range(TILES):
-        blocks.append((t, None))
+    blocks = [(t, None) for t in range(TILES)]
     for w in range(1, WIN):
         t = NT * w // TILE
         blocks.append((t, NT * DECIM * w - SPAN * t))
@@ -177,9 +175,10 @@
         send_ref[z, :, TILE * g : TILE * g + TILE] = both.astype(BF16)
 
 
-def spectra_kernel(x_ref, taps_ref, bins_ref, mask_ref, send_ref, fir_ref, table_ref, left_ref, res_ref, dec_ref):
+def spectra(x_ref, loaded, taps_ref, bins_ref, mask_ref, send_ref, fir_ref, table_ref, left_ref, res_ref, dec_ref):
     build_fir(taps_ref, fir_ref)
     build_table(bins_ref, table_ref)
+    loaded.wait()
     build_left(x_ref, left_ref)
     res_ref[...] = jnp.dot(left_ref[...], fir_ref[...], preferred_element_type=F32)
     align_windows(res_ref, dec_ref)
@@ -192,26 +191,24 @@
     pack(white, send_ref)
 
 
-def spectra(raw_strain, fir_taps, band_bins, live_mask):
-    vmem = pl.BlockSpec(memory_space=pltpu.VMEM)
-    return pl.pallas_call(
-        spectra_kernel,
-        out_shape=jax.ShapeDtypeStruct((4, 16, PACK), BF16),
-        in_specs=[vmem] * 4,
-        out_specs=vmem,
-        scratch_shapes=[
-            pltpu.VMEM((SPAN, 256), BF16),
-            pltpu.VMEM((NTP, 512), BF16),
-            pltpu.VMEM((1024, SPAN), BF16),
-            pltpu.VMEM((1024, 256), F32),
-            pltpu.VMEM((80, NTP), BF16),
-        ],
-        compiler_params=pltpu.CompilerParams(vmem_limit_bytes=32 * 1024 * 1024),
-        name="spectra",
-    )(raw_strain, fir_taps.reshape(1, TAPS), band_bins.reshape(1, BINS), live_mask)
-
-
-def gather_kernel(send_ref, own_ref, all_ref, raw, hold, z_send, z_recv, g_send, g_recv, local_sem):
+PROGRAM = (
+    ("s", 1), ("s", -1), ("s", 2), ("S", 0, 1), ("S", 0, -1), ("H", 0, 0),
+    ("w", 1), ("S", -1, 1), ("S", -1, -1), ("w", -1), ("S", 1, 1), ("S", 1, -1), ("H", -1, 0), ("H", 1, 0),
+    ("w", 2), ("S", 2, 1), ("S", 2, -1), ("S", 2, 2), ("S", -1, 2), ("S", 1, 2), ("H", 2, 0),
+    ("W", 0, 1), ("R", 0, 1), ("W", 0, -1), ("R", 0, -1), ("H", 0, -1), ("H", 0, 1),
+    ("W", -1, 1), ("H", -1, -1), ("W", -1, -1), ("H", -1, 1),
+    ("W", 1, 1), ("H", 1, -1), ("W", 1, -1), ("H", 1, 1),
+    ("W", 2, 1), ("H", 2, -1), ("W", 2, -1), ("H", 2, 1),
+    ("Q", 0), ("H", 0, 2), ("W", 2, 2), ("H", 2, 2), ("W", -1, 2), ("H", -1, 2), ("W", 1, 2), ("H", 1, 2),
+)
+COPIES = 2 * sum(step[0] in "sSRH" for step in PROGRAM)
+
+
+def gather_kernel(
+    x_ref, taps_ref, bins_ref, mask_ref, own_ref, all_ref,
+    x_here, taps_here, bins_here, mask_here, fir_ref, table_ref, left_ref, res_ref, dec_ref, send_ref, raw,
+    in_sem, z_send, z_recv, g_send, g_recv,
+):
     z = lax.axis_index("freq")
     b = lax.axis_index("chan")
     x, y, c = b // 8, (b // 2) % 4, b % 2
@@ -221,16 +218,30 @@
 
     sibling = index(x, y, 1 - c)
     peers = [((z + d) % 4, b) for d in (1, 2, 3)]
-    peers += [(z, index(x + d, y, c)) for d in (1, 3)]
-    peers += [(z, index(x, y + d, c)) for d in (1, 3)]
+    peers += [(z, index(x + d, y, c)) for d in (1, 2, 3)]
+    peers += [(z, index(x, y + d, c)) for d in (1, 2, 3)]
     peers += [(z, sibling)]
     barrier = pltpu.get_barrier_semaphore()
     for peer in peers:
         pl.semaphore_signal(barrier, inc=1, device_id=peer, device_id_type=MESH)
+
+    small = []
+    for at, (src, dst) in enumerate(((taps_ref, taps_here), (bins_ref, bins_here), (mask_ref, mask_here))):
+        copy = pltpu.make_async_copy(src, dst, in_sem.at[at])
+        copy.start()
+        small.append(copy)
+    loaded = pltpu.make_async_copy(x_ref, x_here, in_sem.at[3])
+    loaded.start()
+    for copy in small:
+        copy.wait()
+    spectra(
+        x_here, loaded, taps_here, bins_here, mask_here, send_ref,
+        fir_ref, table_ref, left_ref, res_ref, dec_ref,
+    )
     pl.semaphore_wait(barrier, len(peers))
 
     crossing = []
-    for d in (1, 2, 3):
+    for d in (2, 1, 3):
         to = (z + d) % 4
         copy = pltpu.make_async_remote_copy(
             src_ref=send_ref.at[to], dst_ref=raw.at[z],
@@ -243,184 +254,160 @@
     for copy in crossing:
         copy.wait_recv()
     for pair in range(2):
+        rows = slice(16 * pair, 16 * pair + 16)
         even = raw[2 * pair].astype(F32)
         odd = raw[2 * pair + 1].astype(F32)
         low = jnp.concatenate([even[0:8], odd[0:8]], axis=0).astype(BF16)
         high = jnp.concatenate([even[8:16], odd[8:16]], axis=0).astype(BF16)
-        for g in range(5):
-            hold[16 * pair : 16 * pair + 16, 256 * g : 256 * g + TILE] = low[:, TILE * g : TILE * g + TILE]
-            hold[16 * pair : 16 * pair + 16, 256 * g + TILE : 256 * g + 256] = high[:, TILE * g : TILE * g + TILE]
-
-    own_copy = pltpu.make_async_copy(hold, own_ref, local_sem.at[0])
-    own_copy.start()
-    own_all = pltpu.make_async_copy(hold, all_ref.at[b], local_sem.at[1])
-    own_all.start()
+        for at in range(10):
+            source = high if at % 2 else low
+            piece = source[:, TILE * (at // 2) : TILE * (at // 2) + TILE]
+            lanes = slice(TILE * at, TILE * at + TILE)
+            own_ref[rows, lanes] = piece
+            all_ref[b, rows, lanes] = piece
 
     started = []
     full, first, second = (0, WIDE), (0, WIDE // 2), (WIDE // 2, WIDE // 2)
 
-    def spot(source, half, lanes):
-        return all_ref.at[source, pl.ds(16 * half, 16), pl.ds(*lanes)]
-
-    def push(source, half, lanes, target, held=False):
+    def push(source, half, lanes, target):
         at = len(started)
-        src = hold.at[pl.ds(16 * half, 16), pl.ds(*lanes)] if held else spot(source, half, lanes)
+        spot = all_ref.at[source, pl.ds(16 * half, 16), pl.ds(*lanes)]
         copy = pltpu.make_async_remote_copy(
-            src_ref=src, dst_ref=spot(source, half, lanes),
-            send_sem=g_send.at[at], recv_sem=g_recv.at[at],
+            src_ref=spot, dst_ref=spot, send_sem=g_send.at[at], recv_sem=g_recv.at[at],
             device_id=(z, target), device_id_type=MESH,
         )
         copy.start()
         started.append(copy)
         return copy
 
-    def arrived(copy, source, half, lanes):
+    def block(half, u, v):
+        return index(x + u, y + v, c) if half == 0 else index(x + v, y + u, c)
+
+    def relayed(d):
+        return first if d == 1 else second
+
+    near, far, onward, shares = {}, {}, {}, []
+    for kind, *args in PROGRAM:
+        for half in (0, 1):
+            if kind == "s":
+                near[half, args[0]] = push(b, half, full, block(half, args[0], 0))
+            elif kind == "w":
+                near[half, args[0]].wait_recv()
+            elif kind == "S":
+                u, d = args
+                far[half, u, d] = push(block(half, u, 0), half, full, block(half, 0, d))
+            elif kind == "W":
+                far[(half, *args)].wait_recv()
+            elif kind == "R":
+                u, d = args
+                onward[half, u, d] = push(block(half, u, -d), half, relayed(d), block(half, 0, d))
+            elif kind == "Q":
+                onward[half, args[0], 1].wait_recv()
+                onward[half, args[0], -1].wait_recv()
+            else:
+                shares.append(push(block(half, *args), half, full, sibling))
+    for copy in shares:
         copy.wait_recv()
-
-    def near(half, d):
-        return index(x + d, y, c) if half == 0 else index(x, y + d, c)
-
-    def far(half, d):
-        return index(x, y + d, c) if half == 0 else index(x + d, y, c)
-
-    def block(half, u, v, cc):
-        return index(x + u, y + v, cc) if half == 0 else index(x + v, y + u, cc)
-
-    siblings = []
-
-    def share(half, u, v, held=False):
-        copy = push(block(half, u, v, c), half, full, sibling, held)
-        siblings.append((copy, half, u, v))
-
-    outer = {}
-
-    def spread(half, u, held=False):
-        for d in (1, -1):
-            outer[half, u, d] = push(block(half, u, 0, c), half, full, far(half, d), held)
-
-    one = {}
-    for half in (0, 1):
-        for d in (1, -1):
-            one[half, d] = push(b, half, full, near(half, d), True)
-    for half in (0, 1):
-        spread(half, 0, True)
-        share(half, 0, 0, True)
-    relay = {}
-    for half in (0, 1):
-        for d in (1, -1):
-            source = block(half, -d, 0, c)
-            arrived(one[half, d], source, half, full)
-            relay[half, d] = push(source, half, first if d == 1 else second, near(half, d))
-    for half in (0, 1):
-        for d in (1, -1):
-            spread(half, -d)
-            share(half, -d, 0)
-    onward = {}
-
-    def pass_on(half, u):
-        for d in (1, -1):
-            source = block(half, u, -d, c)
-            arrived(outer[half, u, d], source, half, full)
-            onward[half, u, d] = push(source, half, first if d == 1 else second, far(half, d))
-            share(half, u, -d)
-
-    def finish(half, u):
-        source = block(half, u, 2, c)
-        arrived(onward[half, u, 1], source, half, first)
-        arrived(onward[half, u, -1], source, half, second)
-        share(half, u, 2)
-
-    for half in (0, 1):
-        source = block(half, 2, 0, c)
-        arrived(relay[half, 1], source, half, first)
-        arrived(relay[half, -1], source, half, second)
-        spread(half, 2)
-        share(half, 2, 0)
-    for u in (0, -1, 1, 2):
-        for half in (0, 1):
-            pass_on(half, u)
-    for u in (0, -1, 1, 2):
-        for half in (0, 1):
-            finish(half, u)
-    for copy, half, u, v in siblings:
-        arrived(copy, block(half, u, v, 1 - c), half, full)
-    for copy in started:
+    for copy in started + crossing:
         copy.wait_send()
-    for copy in crossing:
-        copy.wait_send()
-    own_copy.wait()
-    own_all.wait()
-
-
-def gather(send):
+
+
+def gather(raw_strain, fir_taps, band_bins, live_mask):
     vmem = pl.BlockSpec(memory_space=pltpu.VMEM)
-    hbm = pl.BlockSpec(memory_space=pl.ANY)
-    count = 72
+    hbm = pl.BlockSpec(memory_space=pltpu.HBM)
+    arrays = (raw_strain, fir_taps.reshape(1, TAPS), band_bins.reshape(1, BINS), live_mask)
+    arrays = [pltpu.with_memory_space_constraint(one, pltpu.HBM) for one in arrays]
     return pl.pallas_call(
         gather_kernel,
         out_shape=(
             jax.ShapeDtypeStruct((32, WIDE), BF16),
             jax.ShapeDtypeStruct((32, 32, WIDE), BF16),
         ),
-        in_specs=[vmem],
-        out_specs=(hbm, hbm),
+        in_specs=[hbm] * 4,
+        out_specs=(vmem, vmem),
         scratch_shapes=[
+            pltpu.VMEM((1, ROWS, SAMPLES), BF16),
+            pltpu.VMEM((1, TAPS), BF16),
+            pltpu.VMEM((1, BINS), I32),
+            pltpu.VMEM((1, 8), I32),
+            pltpu.VMEM((SPAN, 256), BF16),
+            pltpu.VMEM((NTP, 512), BF16),
+            pltpu.VMEM((1024, SPAN), BF16),
+            pltpu.VMEM((1024, 256), F32),
+            pltpu.VMEM((80, NTP), BF16),
             pltpu.VMEM((4, 16, PACK), BF16),
-            pltpu.VMEM((32, WIDE), BF16),
+            pltpu.VMEM((4, 16, PACK), BF16),
+            pltpu.SemaphoreType.DMA((4,)),
             pltpu.SemaphoreType.DMA((3,)),
             pltpu.SemaphoreType.DMA((3,)),
-            pltpu.SemaphoreType.DMA((count,)),
-            pltpu.SemaphoreType.DMA((count,)),
-            pltpu.SemaphoreType.DMA((2,)),
+            pltpu.SemaphoreType.DMA((COPIES,)),
+            pltpu.SemaphoreType.DMA((COPIES,)),
         ],
         compiler_params=pltpu.CompilerParams(
-            collective_id=0, has_side_effects=True, vmem_limit_bytes=8 * 1024 * 1024
+            collective_id=0, has_side_effects=True, vmem_limit_bytes=32 * 1024 * 1024
         ),
         name="gather",
-    )(send)
-
-
-PER_STEP = 4
-
-
-def correlate_kernel(own_ref, all_ref, out_ref):
-    step = pl.program_id(0) % (GROUP // PER_STEP)
-    own = own_ref[...].astype(F32)
+    )(*arrays)
+
+
+SLOTS = 8
+
+
+def correlate_kernel(own_ref, all_ref, out_ref, left_ref, slot_ref, sem):
     lane = iota((32, 256), 1)
-    turned = jnp.where(
-        lane < 120, pltpu.roll(own, 256 - 120, 1), jnp.where(lane < 240, -pltpu.roll(own, 120, 1), 0.0)
-    )
-    bin_of = lane % GROUP
-    rows = []
-    for f in range(PER_STEP):
-        keep = bin_of == step * PER_STEP + f
-        rows.append(jnp.where(keep, own, 0.0))
-        rows.append(jnp.where(keep, turned, 0.0))
-    left = jnp.concatenate(rows, axis=0).astype(BF16)
-    right = all_ref[...].reshape(1024, 256)
-    prod = lax.dot_general(left, right, (((1,), (1,)), ((), ())), preferred_element_type=F32)
-    out_ref[...] = (prod * (1.0 / WIN)).reshape(PER_STEP, 2, 32, 1024)
+    copies = []
+    for g in range(5):
+        lanes = slice(256 * g, 256 * g + 256)
+        own = own_ref[:, lanes].astype(F32)
+        turned = jnp.where(
+            lane < 120,
+            pltpu.roll(own, 256 - 120, 1),
+            jnp.where(lane < 240, -pltpu.roll(own, 120, 1), 0.0),
+        )
+        for f in range(GROUP):
+            keep = lane % GROUP == f
+            both = jnp.concatenate([jnp.where(keep, own, 0.0), jnp.where(keep, turned, 0.0)], axis=0)
+            left_ref[64 * f : 64 * f + 64, :] = both.astype(BF16)
+        for part in range(4):
+            at = len(copies)
+            slot = at % SLOTS
+            if at >= SLOTS:
+                copies[at - SLOTS].wait()
+            right = all_ref[8 * part : 8 * part + 8, :, lanes].reshape(256, 256)
+            prod = lax.dot_general(
+                left_ref[...], right, (((1,), (1,)), ((), ())), preferred_element_type=F32
+            )
+            slot_ref[slot] = (prod * (1.0 / WIN)).reshape(GROUP, 2, 32, 256)
+            copy = pltpu.make_async_copy(
+                slot_ref.at[slot],
+                out_ref.at[pl.ds(GROUP * g, GROUP), :, :, pl.ds(256 * part, 256)],
+                sem.at[slot],
+            )
+            copy.start()
+            copies.append(copy)
+    for copy in copies[-SLOTS:]:
+        copy.wait()
 
 
 def correlate(own, everyone):
-    per_group = GROUP // PER_STEP
+    vmem = pl.BlockSpec(memory_space=pltpu.VMEM)
     return pl.pallas_call(
         correlate_kernel,
         out_shape=jax.ShapeDtypeStruct((60, 2, 32, 1024), F32),
-        grid=(60 // PER_STEP,),
-        in_specs=[
-            pl.BlockSpec((32, 256), lambda i: (0, i // per_group)),
-            pl.BlockSpec((32, 32, 256), lambda i: (0, 0, i // per_group)),
+        in_specs=[vmem, vmem],
+        out_specs=pl.BlockSpec(memory_space=pltpu.HBM),
+        scratch_shapes=[
+            pltpu.VMEM((64 * GROUP, 256), BF16),
+            pltpu.VMEM((SLOTS, GROUP, 2, 32, 256), F32),
+            pltpu.SemaphoreType.DMA((SLOTS,)),
         ],
-        out_specs=pl.BlockSpec((PER_STEP, 2, 32, 1024), lambda i: (i, 0, 0, 0)),
         compiler_params=pltpu.CompilerParams(vmem_limit_bytes=32 * 1024 * 1024),
         name="correlate",
     )(own, everyone)
 
 
 def shards(raw_strain, fir_taps, band_bins, live_mask):
-    send = spectra(raw_strain, fir_taps, band_bins, live_mask)
-    own, everyone = gather(send)
+    own, everyone = gather(raw_strain, fir_taps, band_bins, live_mask)
     return correlate(own, everyone)
 
 

time: 45.1 us -> 33.3 us (0.74)
  Pallas kernels: 41.2 us -> 33.1 us
  local copies, waits for them, and re-layouts: 3.66 us -> 0 us
    pallas_call x1, Pallas kernels: 10.7 us -> 6.91 us  [correlate(): pl.pallas_call(correlate_kernel, out_shape=jax.ShapeDtypeStruct((60, 2, 3...]
    unnamed x8 -> x0, local copies, waits for them, and re-layouts: 3.66 us -> none
    pallas_call x1, Pallas kernels: 28.4 us -> 26.2 us  [gather(): pl.pallas_call(gather_kernel, out_shape=(jax.ShapeDtypeStruct((32, WIDE),...]
    pallas_call x1 -> x0, Pallas kernels: 2.14 us -> none  [spectra(): pl.pallas_call(spectra_kernel, out_shape=jax.ShapeDtypeStruct((4, 16, PAC...]
where the time goes in v2:
time: 33.3 us; the launch traced here: 33.1 us
  Pallas kernels  33.1 us (99%)
    pallas_call x1, Pallas kernels, gather(): pl.pallas_call(gather_kernel, out_shape=(jax.ShapeDtypeStruct((32, WIDE),...  26.2 us
    pallas_call x1, Pallas kernels, correlate(): pl.pallas_call(correlate_kernel, out_shape=jax.ShapeDtypeStruct((60, 2, 3...  6.91 us

profile of v2, /device:TPU:1, one launch (start us, length us, event | category | flops | bytes accessed | tf_op | source)
XLA Modules:
  0.0 33.1 jit_solution(2801364000172758562)
XLA Ops:
  0.0 26.2 %gather.1 = (bf16[32,1280]{1,0:T(8,128)(2,1)S(1)}, bf16[32,32,1280]{2,1,0:T(8,128)(2,1)S(1)}) custom-call(bf16[1,8,150000]{2,1,0:T(8,128)(2,1)} %x_ref.1, bf16[1,20]{1,0:T(2,128)(2,1)} %bitcast.3, s32[1,240]{1,0:T(1,128)} %bitcast.2, s32[1,8]{1,0:T(1,128)} %mask_ref.1), custom_call_target="tpu_custom_call" | custom-call | tf_op jit(solution)/shard_map/gather/pallas_call | solution.py:320
  26.2 6.9 %correlate.1 = f32[60,2,32,1024]{3,2,1,0:T(8,128)} custom-call(bf16[32,1280]{1,0:T(8,128)(2,1)S(1)} %get-tuple-element.7.own_ref, bf16[32,32,1280]{2,1,0:T(8,128)(2,1)S(1)} %get-tuple-element.8.all_ref), custom_call_target="tpu_custom_call" | custom-call | tf_op jit(solution)/shard_map/correlate/pallas_call | solution.py:394

commit v3 on v2

--- a/solution.py
+++ b/solution.py
@@ -191,17 +191,7 @@
     pack(white, send_ref)
 
 
-PROGRAM = (
-    ("s", 1), ("s", -1), ("s", 2), ("S", 0, 1), ("S", 0, -1), ("H", 0, 0),
-    ("w", 1), ("S", -1, 1), ("S", -1, -1), ("w", -1), ("S", 1, 1), ("S", 1, -1), ("H", -1, 0), ("H", 1, 0),
-    ("w", 2), ("S", 2, 1), ("S", 2, -1), ("S", 2, 2), ("S", -1, 2), ("S", 1, 2), ("H", 2, 0),
-    ("W", 0, 1), ("R", 0, 1), ("W", 0, -1), ("R", 0, -1), ("H", 0, -1), ("H", 0, 1),
-    ("W", -1, 1), ("H", -1, -1), ("W", -1, -1), ("H", -1, 1),
-    ("W", 1, 1), ("H", 1, -1), ("W", 1, -1), ("H", 1, 1),
-    ("W", 2, 1), ("H", 2, -1), ("W", 2, -1), ("H", 2, 1),
-    ("Q", 0), ("H", 0, 2), ("W", 2, 2), ("H", 2, 2), ("W", -1, 2), ("H", -1, 2), ("W", 1, 2), ("H", 1, 2),
-)
-COPIES = 2 * sum(step[0] in "sSRH" for step in PROGRAM)
+COPIES = 4 * (3 + 12 + 4)
 
 
 def gather_kernel(
@@ -240,7 +230,7 @@
     )
     pl.semaphore_wait(barrier, len(peers))
 
-    crossing = []
+    crossing, landed = [], {}
     for d in (2, 1, 3):
         to = (z + d) % 4
         copy = pltpu.make_async_remote_copy(
@@ -250,13 +240,46 @@
         )
         copy.start()
         crossing.append(copy)
+        landed[d] = copy
     raw[z] = send_ref[z]
-    for copy in crossing:
-        copy.wait_recv()
-    for pair in range(2):
-        rows = slice(16 * pair, 16 * pair + 16)
-        even = raw[2 * pair].astype(F32)
-        odd = raw[2 * pair + 1].astype(F32)
+
+    started, shares = [], []
+
+    def push(region, target):
+        at = len(started)
+        copy = pltpu.make_async_remote_copy(
+            src_ref=region, dst_ref=region, send_sem=g_send.at[at], recv_sem=g_recv.at[at],
+            device_id=(z, target), device_id_type=MESH,
+        )
+        copy.start()
+        started.append(copy)
+        return copy
+
+    def place(route, u, v):
+        return ((x + u) % 4, (y + v) % 4) if route == 0 else ((x + v) % 4, (y + u) % 4)
+
+    def part(half, route):
+        return pl.ds(16 * half, 16), pl.ds(PACK * route, PACK)
+
+    def send(half, route, u, u_to, v_to):
+        xx, yy = place(route, u, 0)
+        region = all_ref.at[(xx, yy, c) + part(half, route)]
+        return push(region, index(*place(route, u_to, v_to), c))
+
+    def share(half, route, u):
+        xx, yy = place(route, u, 0)
+        if route == 0:
+            region = all_ref.at[(xx, slice(None), c) + part(half, route)]
+        else:
+            region = all_ref.at[(slice(None), yy, c) + part(half, route)]
+        shares.append(push(region, sibling))
+
+    near, far = {}, {}
+
+    def unite(half):
+        rows = slice(16 * half, 16 * half + 16)
+        even = raw[2 * half].astype(F32)
+        odd = raw[2 * half + 1].astype(F32)
         low = jnp.concatenate([even[0:8], odd[0:8]], axis=0).astype(BF16)
         high = jnp.concatenate([even[8:16], odd[8:16]], axis=0).astype(BF16)
         for at in range(10):
@@ -264,48 +287,49 @@
             piece = source[:, TILE * (at // 2) : TILE * (at // 2) + TILE]
             lanes = slice(TILE * at, TILE * at + TILE)
             own_ref[rows, lanes] = piece
-            all_ref[b, rows, lanes] = piece
-
-    started = []
-    full, first, second = (0, WIDE), (0, WIDE // 2), (WIDE // 2, WIDE // 2)
-
-    def push(source, half, lanes, target):
-        at = len(started)
-        spot = all_ref.at[source, pl.ds(16 * half, 16), pl.ds(*lanes)]
-        copy = pltpu.make_async_remote_copy(
-            src_ref=spot, dst_ref=spot, send_sem=g_send.at[at], recv_sem=g_recv.at[at],
-            device_id=(z, target), device_id_type=MESH,
-        )
-        copy.start()
-        started.append(copy)
-        return copy
-
-    def block(half, u, v):
-        return index(x + u, y + v, c) if half == 0 else index(x + v, y + u, c)
-
-    def relayed(d):
-        return first if d == 1 else second
-
-    near, far, onward, shares = {}, {}, {}, []
-    for kind, *args in PROGRAM:
-        for half in (0, 1):
-            if kind == "s":
-                near[half, args[0]] = push(b, half, full, block(half, args[0], 0))
-            elif kind == "w":
-                near[half, args[0]].wait_recv()
-            elif kind == "S":
-                u, d = args
-                far[half, u, d] = push(block(half, u, 0), half, full, block(half, 0, d))
-            elif kind == "W":
-                far[(half, *args)].wait_recv()
-            elif kind == "R":
-                u, d = args
-                onward[half, u, d] = push(block(half, u, -d), half, relayed(d), block(half, 0, d))
-            elif kind == "Q":
-                onward[half, args[0], 1].wait_recv()
-                onward[half, args[0], -1].wait_recv()
-            else:
-                shares.append(push(block(half, *args), half, full, sibling))
+            all_ref[x, y, c, rows, lanes] = piece
+
+    def begin(half):
+        for d in (1, -1, 2):
+            for route in (0, 1):
+                near[half, route, d] = send(half, route, 0, d, 0)
+        for d in (1, -1, 2):
+            for route in (0, 1):
+                far[half, route, 0, d] = send(half, route, 0, 0, d)
+
+    def go_on(half):
+        for d in (1, -1, 2):
+            u = d if d == 2 else -d
+            for route in (0, 1):
+                near[half, route, d].wait_recv()
+                for v in (1, -1, 2):
+                    far[half, route, u, v] = send(half, route, u, 0, v)
+
+    def finish(half):
+        for u in (0, -1, 1, 2):
+            for route in (0, 1):
+                for v in (1, -1, 2):
+                    far[half, route, u, v].wait_recv()
+                share(half, route, u)
+
+    def arrive(source):
+        for d in (1, 2, 3):
+            @pl.when((z - source + 4) % 4 == d)
+            def _():
+                landed[d].wait_recv()
+
+    arrive(0)
+    arrive(1)
+    unite(0)
+    begin(0)
+    arrive(2)
+    arrive(3)
+    unite(1)
+    begin(1)
+    go_on(0)
+    go_on(1)
+    finish(0)
+    finish(1)
     for copy in shares:
         copy.wait_recv()
     for copy in started + crossing:
@@ -321,7 +345,7 @@
         gather_kernel,
         out_shape=(
             jax.ShapeDtypeStruct((32, WIDE), BF16),
-            jax.ShapeDtypeStruct((32, 32, WIDE), BF16),
+            jax.ShapeDtypeStruct((4, 4, 2, 32, WIDE), BF16),
         ),
         in_specs=[hbm] * 4,
         out_specs=(vmem, vmem),
@@ -408,7 +432,7 @@
 
 def shards(raw_strain, fir_taps, band_bins, live_mask):
     own, everyone = gather(raw_strain, fir_taps, band_bins, live_mask)
-    return correlate(own, everyone)
+    return correlate(own, everyone.reshape(32, 32, WIDE))
 
 
 def solution(mesh):

time: 33.3 us -> 31.8 us (0.955)
  Pallas kernels: 33.1 us -> 31.6 us
    pallas_call x1, Pallas kernels: 26.2 us -> 24.7 us  [gather(): pl.pallas_call(gather_kernel, out_shape=(jax.ShapeDtypeStruct((32, WIDE),...]
where the time goes in v3:
time: 31.8 us; the launch traced here: 31.6 us
  Pallas kernels  31.6 us (99%)
    pallas_call x1, Pallas kernels, gather(): pl.pallas_call(gather_kernel, out_shape=(jax.ShapeDtypeStruct((32, WIDE),...  24.7 us
    pallas_call x1, Pallas kernels, correlate(): pl.pallas_call(correlate_kernel, out_shape=jax.ShapeDtypeStruct((60, 2, 3...  6.91 us

profile of v3, /device:TPU:1, one launch (start us, length us, event | category | flops | bytes accessed | tf_op | source)
XLA Modules:
  0.0 31.6 jit_solution(16743398929476508532)
XLA Ops:
  0.0 24.7 %gather.1 = (bf16[32,1280]{1,0:T(8,128)(2,1)S(1)}, bf16[4,4,2,32,1280]{4,3,2,1,0:T(8,128)(2,1)S(1)}) custom-call(bf16[1,8,150000]{2,1,0:T(8,128)(2,1)} %x_ref.1, bf16[1,20]{1,0:T(2,128)(2,1)} %bitcast.5, s32[1,240]{1,0:T(1,128)} %bitcast.4, s32[1,8]{1,0:T(1,128)} %mask_ref.1), custom_call_target="tpu_custom_call" | custom-call | tf_op jit(solution)/shard_map/gather/pallas_call | solution.py:344
  24.7 6.9 %correlate.1 = f32[60,2,32,1024]{3,2,1,0:T(8,128)} custom-call(bf16[32,1280]{1,0:T(8,128)(2,1)S(1)} %get-tuple-element.7.own_ref, bf16[32,32,1280]{2,1,0:T(8,128)(2,1)S(1)} %bitcast.3), custom_call_target="tpu_custom_call" | custom-call | tf_op jit(solution)/shard_map/correlate/pallas_call | solution.py:418

commit v4 on v3

--- a/solution.py
+++ b/solution.py
@@ -191,7 +191,41 @@
     pack(white, send_ref)
 
 
-COPIES = 4 * (3 + 12 + 4)
+def schedule():
+    steps = []
+
+    def begin(h):
+        for d in (1, -1, 2):
+            steps.append(("near", h, d))
+        for v in (1, -1, 2):
+            steps.append(("far", h, 0, v))
+
+    def go_on(h):
+        for d in (1, -1, 2):
+            u = d if d == 2 else -d
+            steps.append(("near_wait", h, d))
+            for v in (1, -1, 2):
+                steps.append(("far", h, u, v))
+
+    def finish(h):
+        for u in (0, -1, 1, 2):
+            for v in (1, -1, 2):
+                steps.append(("far_wait", h, u, v))
+            steps.append(("share", h, u))
+
+    steps.append(("take", 0))
+    begin(0)
+    steps.append(("take", 1))
+    begin(1)
+    go_on(0)
+    go_on(1)
+    finish(0)
+    finish(1)
+    return steps
+
+
+SCHEDULE = schedule()
+COPIES = 2 * sum(step[0] in ("near", "far", "relay", "share") for step in SCHEDULE)
 
 
 def gather_kernel(
@@ -289,47 +323,38 @@
             own_ref[rows, lanes] = piece
             all_ref[x, y, c, rows, lanes] = piece
 
-    def begin(half):
-        for d in (1, -1, 2):
-            for route in (0, 1):
-                near[half, route, d] = send(half, route, 0, d, 0)
-        for d in (1, -1, 2):
-            for route in (0, 1):
-                far[half, route, 0, d] = send(half, route, 0, 0, d)
-
-    def go_on(half):
-        for d in (1, -1, 2):
-            u = d if d == 2 else -d
-            for route in (0, 1):
-                near[half, route, d].wait_recv()
-                for v in (1, -1, 2):
-                    far[half, route, u, v] = send(half, route, u, 0, v)
-
-    def finish(half):
-        for u in (0, -1, 1, 2):
-            for route in (0, 1):
-                for v in (1, -1, 2):
-                    far[half, route, u, v].wait_recv()
-                share(half, route, u)
-
     def arrive(source):
         for d in (1, 2, 3):
             @pl.when((z - source + 4) % 4 == d)
             def _():
                 landed[d].wait_recv()
 
-    arrive(0)
-    arrive(1)
-    unite(0)
-    begin(0)
-    arrive(2)
-    arrive(3)
-    unite(1)
-    begin(1)
-    go_on(0)
-    go_on(1)
-    finish(0)
-    finish(1)
+    relayed = {}
+    for kind, half, *rest in SCHEDULE:
+        if kind == "take":
+            arrive(2 * half)
+            arrive(2 * half + 1)
+            unite(half)
+            continue
+        for route in (0, 1):
+            if kind == "near":
+                near[half, route, rest[0]] = send(half, route, 0, rest[0], 0)
+            elif kind == "far":
+                u, v = rest
+                far[half, route, u, v] = send(half, route, u, 0, v)
+            elif kind == "near_wait":
+                near[half, route, rest[0]].wait_recv()
+            elif kind == "far_wait":
+                far[(half, route, *rest)].wait_recv()
+            elif kind == "relay":
+                u, v = rest
+                xx, yy = place(route, u, -v)
+                region = all_ref.at[(xx, yy, c) + part(half, route)]
+                relayed[half, route, u] = push(region, index(*place(route, 0, v), c))
+            elif kind == "relay_wait":
+                relayed[half, route, rest[0]].wait_recv()
+            else:
+                share(half, route, rest[0])
     for copy in shares:
         copy.wait_recv()
     for copy in started + crossing:
@@ -375,6 +400,7 @@
 
 
 SLOTS = 8
+STEP = 4
 
 
 def correlate_kernel(own_ref, all_ref, out_ref, left_ref, slot_ref, sem):
@@ -392,20 +418,17 @@
             keep = lane % GROUP == f
             both = jnp.concatenate([jnp.where(keep, own, 0.0), jnp.where(keep, turned, 0.0)], axis=0)
             left_ref[64 * f : 64 * f + 64, :] = both.astype(BF16)
-        for part in range(4):
+        right = all_ref[:, :, lanes].reshape(1024, 256)
+        for first in range(0, GROUP, STEP):
             at = len(copies)
             slot = at % SLOTS
             if at >= SLOTS:
                 copies[at - SLOTS].wait()
-            right = all_ref[8 * part : 8 * part + 8, :, lanes].reshape(256, 256)
-            prod = lax.dot_general(
-                left_ref[...], right, (((1,), (1,)), ((), ())), preferred_element_type=F32
-            )
-            slot_ref[slot] = (prod * (1.0 / WIN)).reshape(GROUP, 2, 32, 256)
+            left = left_ref[64 * first : 64 * (first + STEP), :]
+            prod = lax.dot_general(left, right, (((1,), (1,)), ((), ())), preferred_element_type=F32)
+            slot_ref[slot] = (prod * (1.0 / WIN)).reshape(STEP, 2, 32, 1024)
             copy = pltpu.make_async_copy(
-                slot_ref.at[slot],
-                out_ref.at[pl.ds(GROUP * g, GROUP), :, :, pl.ds(256 * part, 256)],
-                sem.at[slot],
+                slot_ref.at[slot], out_ref.at[pl.ds(GROUP * g + first, STEP)], sem.at[slot]
             )
             copy.start()
             copies.append(copy)
@@ -422,7 +445,7 @@
         out_specs=pl.BlockSpec(memory_space=pltpu.HBM),
         scratch_shapes=[
             pltpu.VMEM((64 * GROUP, 256), BF16),
-            pltpu.VMEM((SLOTS, GROUP, 2, 32, 256), F32),
+            pltpu.VMEM((SLOTS, STEP, 2, 32, 1024), F32),
             pltpu.SemaphoreType.DMA((SLOTS,)),
         ],
         compiler_params=pltpu.CompilerParams(vmem_limit_bytes=32 * 1024 * 1024),

time: 31.8 us -> 30.9 us (0.972)
  Pallas kernels: 31.6 us -> 30.7 us
    pallas_call x1, Pallas kernels: 6.91 us -> 5.92 us  [correlate(): pl.pallas_call(correlate_kernel, out_shape=jax.ShapeDtypeStruct((60, 2, 3...]
where the time goes in v4:
time: 30.9 us; the launch traced here: 30.7 us
  Pallas kernels  30.7 us (99%)
    pallas_call x1, Pallas kernels, gather(): pl.pallas_call(gather_kernel, out_shape=(jax.ShapeDtypeStruct((32, WIDE),...  24.8 us
    pallas_call x1, Pallas kernels, correlate(): pl.pallas_call(correlate_kernel, out_shape=jax.ShapeDtypeStruct((60, 2, 3...  5.92 us

profile of v4, /device:TPU:1, one launch (start us, length us, event | category | flops | bytes accessed | tf_op | source)
XLA Modules:
  0.0 30.7 jit_solution(5958252977776402337)
XLA Ops:
  0.0 24.8 %gather.1 = (bf16[32,1280]{1,0:T(8,128)(2,1)S(1)}, bf16[4,4,2,32,1280]{4,3,2,1,0:T(8,128)(2,1)S(1)}) custom-call(bf16[1,8,150000]{2,1,0:T(8,128)(2,1)} %x_ref.1, bf16[1,20]{1,0:T(2,128)(2,1)} %bitcast.5, s32[1,240]{1,0:T(1,128)} %bitcast.4, s32[1,8]{1,0:T(1,128)} %mask_ref.1), custom_call_target="tpu_custom_call" | custom-call | tf_op jit(solution)/shard_map/gather/pallas_call | solution.py:369
  24.8 5.9 %correlate.1 = f32[60,2,32,1024]{3,2,1,0:T(8,128)} custom-call(bf16[32,1280]{1,0:T(8,128)(2,1)S(1)} %get-tuple-element.7.own_ref, bf16[32,32,1280]{2,1,0:T(8,128)(2,1)S(1)} %bitcast.3), custom_call_target="tpu_custom_call" | custom-call | tf_op jit(solution)/shard_map/correlate/pallas_call | solution.py:441

commit v5 on v4

--- a/solution.py
+++ b/solution.py
@@ -209,8 +209,7 @@
 
     def finish(h):
         for u in (0, -1, 1, 2):
-            for v in (1, -1, 2):
-                steps.append(("far_wait", h, u, v))
+            steps.append(("far_wait", h, u))
             steps.append(("share", h, u))
 
     steps.append(("take", 0))
@@ -220,18 +219,18 @@
     go_on(0)
     go_on(1)
     finish(0)
+    steps.append(("drain", 0))
     finish(1)
     return steps
 
 
 SCHEDULE = schedule()
-COPIES = 2 * sum(step[0] in ("near", "far", "relay", "share") for step in SCHEDULE)
 
 
 def gather_kernel(
     x_ref, taps_ref, bins_ref, mask_ref, own_ref, all_ref,
     x_here, taps_here, bins_here, mask_here, fir_ref, table_ref, left_ref, res_ref, dec_ref, send_ref, raw,
-    in_sem, z_send, z_recv, g_send, g_recv,
+    in_sem, z_send, z_recv, sent_sem, near_recv, far_recv, share_sem,
 ):
     z = lax.axis_index("freq")
     b = lax.axis_index("chan")
@@ -277,38 +276,39 @@
         landed[d] = copy
     raw[z] = send_ref[z]
 
-    started, shares = [], []
-
-    def push(region, target):
-        at = len(started)
-        copy = pltpu.make_async_remote_copy(
-            src_ref=region, dst_ref=region, send_sem=g_send.at[at], recv_sem=g_recv.at[at],
+    def push(region, target, sent, landed):
+        pltpu.make_async_remote_copy(
+            src_ref=region, dst_ref=region, send_sem=sent, recv_sem=landed,
             device_id=(z, target), device_id_type=MESH,
-        )
-        copy.start()
-        started.append(copy)
-        return copy
-
-    def place(route, u, v):
-        return ((x + u) % 4, (y + v) % 4) if route == 0 else ((x + v) % 4, (y + u) % 4)
+        ).start()
+
+    def wait_for(region, sem):
+        pltpu.make_async_copy(region, region, sem).wait()
+
+    xs = {d: lax.rem(x + d % 4, 4) for d in (0, 1, -1, 2)}
+    ys = {d: lax.rem(y + d % 4, 4) for d in (0, 1, -1, 2)}
+    along_x = {d: (xs[d] * 4 + y) * 2 + c for d in (1, -1, 2)}
+    along_y = {d: (x * 4 + ys[d]) * 2 + c for d in (1, -1, 2)}
 
     def part(half, route):
         return pl.ds(16 * half, 16), pl.ds(PACK * route, PACK)
 
-    def send(half, route, u, u_to, v_to):
-        xx, yy = place(route, u, 0)
-        region = all_ref.at[(xx, yy, c) + part(half, route)]
-        return push(region, index(*place(route, u_to, v_to), c))
+    def block(half, route, u):
+        xx, yy = (xs[u], y) if route == 0 else (x, ys[u])
+        return all_ref.at[(xx, yy, c) + part(half, route)]
 
     def share(half, route, u):
-        xx, yy = place(route, u, 0)
         if route == 0:
-            region = all_ref.at[(xx, slice(None), c) + part(half, route)]
+            region = all_ref.at[(xs[u], slice(None), c) + part(half, route)]
         else:
-            region = all_ref.at[(slice(None), yy, c) + part(half, route)]
-        shares.append(push(region, sibling))
-
-    near, far = {}, {}
+            region = all_ref.at[(slice(None), ys[u], c) + part(half, route)]
+        push(region, sibling, sent_sem.at[2], share_sem.at[0])
+
+    def near_sem(half, route, d):
+        return near_recv.at[6 * half + 3 * route + (1, -1, 2).index(d)]
+
+    def far_sem(half, route, u):
+        return far_recv.at[8 * half + 4 * route + u % 4]
 
     def unite(half):
         rows = slice(16 * half, 16 * half + 16)
@@ -329,36 +329,35 @@
             def _():
                 landed[d].wait_recv()
 
-    relayed = {}
     for kind, half, *rest in SCHEDULE:
         if kind == "take":
             arrive(2 * half)
             arrive(2 * half + 1)
             unite(half)
             continue
+        if kind == "drain":
+            wait_for(all_ref.at[0, pl.ds(0, 3), 0], sent_sem.at[0])
+            wait_for(all_ref.at[pl.ds(0, 3), :, 0], sent_sem.at[1])
+            for copy in crossing:
+                copy.wait_send()
+            continue
         for route in (0, 1):
             if kind == "near":
-                near[half, route, rest[0]] = send(half, route, 0, rest[0], 0)
+                to = (along_x if route == 0 else along_y)[rest[0]]
+                push(block(half, route, 0), to, sent_sem.at[0], near_sem(half, route, rest[0]))
+            elif kind == "near_wait":
+                wait_for(block(half, route, 0), near_sem(half, route, rest[0]))
             elif kind == "far":
                 u, v = rest
-                far[half, route, u, v] = send(half, route, u, 0, v)
-            elif kind == "near_wait":
-                near[half, route, rest[0]].wait_recv()
+                to = (along_y if route == 0 else along_x)[v]
+                push(block(half, route, u), to, sent_sem.at[1], far_sem(half, route, u))
             elif kind == "far_wait":
-                far[(half, route, *rest)].wait_recv()
-            elif kind == "relay":
-                u, v = rest
-                xx, yy = place(route, u, -v)
-                region = all_ref.at[(xx, yy, c) + part(half, route)]
-                relayed[half, route, u] = push(region, index(*place(route, 0, v), c))
-            elif kind == "relay_wait":
-                relayed[half, route, rest[0]].wait_recv()
+                three = all_ref.at[(pl.ds(0, 3), 0, 0) + part(half, route)]
+                wait_for(three, far_sem(half, route, rest[0]))
             else:
                 share(half, route, rest[0])
-    for copy in shares:
-        copy.wait_recv()
-    for copy in started + crossing:
-        copy.wait_send()
+    wait_for(all_ref.at[:, :, 0], share_sem.at[0])
+    wait_for(all_ref.at[:, :, 0], sent_sem.at[2])
 
 
 def gather(raw_strain, fir_taps, band_bins, live_mask):
@@ -389,8 +388,10 @@
             pltpu.SemaphoreType.DMA((4,)),
             pltpu.SemaphoreType.DMA((3,)),
             pltpu.SemaphoreType.DMA((3,)),
-            pltpu.SemaphoreType.DMA((COPIES,)),
-            pltpu.SemaphoreType.DMA((COPIES,)),
+            pltpu.SemaphoreType.DMA((3,)),
+            pltpu.SemaphoreType.DMA((12,)),
+            pltpu.SemaphoreType.DMA((16,)),
+            pltpu.SemaphoreType.DMA((1,)),
         ],
         compiler_params=pltpu.CompilerParams(
             collective_id=0, has_side_effects=True, vmem_limit_bytes=32 * 1024 * 1024

time: 30.9 us -> 29.7 us (0.961)
  Pallas kernels: 30.7 us -> 29.5 us
    pallas_call x1, Pallas kernels: 24.8 us -> 23.6 us  [gather(): pl.pallas_call(gather_kernel, out_shape=(jax.ShapeDtypeStruct((32, WIDE),...]
where the time goes in v5:
time: 29.7 us; the launch traced here: 29.5 us
  Pallas kernels  29.5 us (99%)
    pallas_call x1, Pallas kernels, gather(): pl.pallas_call(gather_kernel, out_shape=(jax.ShapeDtypeStruct((32, WIDE),...  23.6 us
    pallas_call x1, Pallas kernels, correlate(): pl.pallas_call(correlate_kernel, out_shape=jax.ShapeDtypeStruct((60, 2, 3...  5.92 us

profile of v5, /device:TPU:1, one launch (start us, length us, event | category | flops | bytes accessed | tf_op | source)
XLA Modules:
  0.0 29.5 jit_solution(515710862820597765)
XLA Ops:
  0.0 23.6 %gather.1 = (bf16[32,1280]{1,0:T(8,128)(2,1)S(1)}, bf16[4,4,2,32,1280]{4,3,2,1,0:T(8,128)(2,1)S(1)}) custom-call(bf16[1,8,150000]{2,1,0:T(8,128)(2,1)} %x_ref.1, bf16[1,20]{1,0:T(2,128)(2,1)} %bitcast.5, s32[1,240]{1,0:T(1,128)} %bitcast.4, s32[1,8]{1,0:T(1,128)} %mask_ref.1), custom_call_target="tpu_custom_call" | custom-call | tf_op jit(solution)/shard_map/gather/pallas_call | solution.py:368
  23.6 5.9 %correlate.1 = f32[60,2,32,1024]{3,2,1,0:T(8,128)} custom-call(bf16[32,1280]{1,0:T(8,128)(2,1)S(1)} %get-tuple-element.7.own_ref, bf16[32,32,1280]{2,1,0:T(8,128)(2,1)S(1)} %bitcast.3), custom_call_target="tpu_custom_call" | custom-call | tf_op jit(solution)/shard_map/correlate/pallas_call | solution.py:442

commit v6 on v5

--- a/solution.py
+++ b/solution.py
@@ -420,19 +420,23 @@
             both = jnp.concatenate([jnp.where(keep, own, 0.0), jnp.where(keep, turned, 0.0)], axis=0)
             left_ref[64 * f : 64 * f + 64, :] = both.astype(BF16)
         right = all_ref[:, :, lanes].reshape(1024, 256)
-        for first in range(0, GROUP, STEP):
+        first = 0
+        for step in (2, 2, 4, 4) if g == 0 else (4, 4, 4):
             at = len(copies)
             slot = at % SLOTS
             if at >= SLOTS:
                 copies[at - SLOTS].wait()
-            left = left_ref[64 * first : 64 * (first + STEP), :]
+            left = left_ref[64 * first : 64 * (first + step), :]
             prod = lax.dot_general(left, right, (((1,), (1,)), ((), ())), preferred_element_type=F32)
-            slot_ref[slot] = (prod * (1.0 / WIN)).reshape(STEP, 2, 32, 1024)
+            slot_ref[slot, 0:step] = (prod * (1.0 / WIN)).reshape(step, 2, 32, 1024)
             copy = pltpu.make_async_copy(
-                slot_ref.at[slot], out_ref.at[pl.ds(GROUP * g + first, STEP)], sem.at[slot]
+                slot_ref.at[slot, pl.ds(0, step)],
+                out_ref.at[pl.ds(GROUP * g + first, step)],
+                sem.at[slot],
             )
             copy.start()
             copies.append(copy)
+            first += step
     for copy in copies[-SLOTS:]:
         copy.wait()
 

time: 29.7 us -> 29.7 us (level)
  no operation moved by 1% of the time
where the time goes in v6:
time: 29.7 us; the launch traced here: 29.5 us
  Pallas kernels  29.5 us (99%)
    pallas_call x1, Pallas kernels, gather(): pl.pallas_call(gather_kernel, out_shape=(jax.ShapeDtypeStruct((32, WIDE),...  23.6 us
    pallas_call x1, Pallas kernels, correlate(): pl.pallas_call(correlate_kernel, out_shape=jax.ShapeDtypeStruct((60, 2, 3...  5.91 us

profile of v6, /device:TPU:1, one launch (start us, length us, event | category | flops | bytes accessed | tf_op | source)
XLA Modules:
  0.0 29.5 jit_solution(2095947854203467746)
XLA Ops:
  0.0 23.6 %gather.1 = (bf16[32,1280]{1,0:T(8,128)(2,1)S(1)}, bf16[4,4,2,32,1280]{4,3,2,1,0:T(8,128)(2,1)S(1)}) custom-call(bf16[1,8,150000]{2,1,0:T(8,128)(2,1)} %x_ref.1, bf16[1,20]{1,0:T(2,128)(2,1)} %bitcast.5, s32[1,240]{1,0:T(1,128)} %bitcast.4, s32[1,8]{1,0:T(1,128)} %mask_ref.1), custom_call_target="tpu_custom_call" | custom-call | tf_op jit(solution)/shard_map/gather/pallas_call | solution.py:368
  23.6 5.9 %correlate.1 = f32[60,2,32,1024]{3,2,1,0:T(8,128)} custom-call(bf16[32,1280]{1,0:T(8,128)(2,1)S(1)} %get-tuple-element.7.own_ref, bf16[32,32,1280]{2,1,0:T(8,128)(2,1)S(1)} %bitcast.3), custom_call_target="tpu_custom_call" | custom-call | tf_op jit(solution)/shard_map/correlate/pallas_call | solution.py:446

commit v7 on v5

--- a/solution.py
+++ b/solution.py
@@ -177,9 +177,9 @@
 
 def spectra(x_ref, loaded, taps_ref, bins_ref, mask_ref, send_ref, fir_ref, table_ref, left_ref, res_ref, dec_ref):
     build_fir(taps_ref, fir_ref)
-    build_table(bins_ref, table_ref)
     loaded.wait()
     build_left(x_ref, left_ref)
+    build_table(bins_ref, table_ref)
     res_ref[...] = jnp.dot(left_ref[...], fir_ref[...], preferred_element_type=F32)
     align_windows(res_ref, dec_ref)
     spectrum = jnp.dot(dec_ref[...], table_ref[...], preferred_element_type=F32)
@@ -248,13 +248,13 @@
     for peer in peers:
         pl.semaphore_signal(barrier, inc=1, device_id=peer, device_id_type=MESH)
 
+    loaded = pltpu.make_async_copy(x_ref, x_here, in_sem.at[3])
+    loaded.start()
     small = []
     for at, (src, dst) in enumerate(((taps_ref, taps_here), (bins_ref, bins_here), (mask_ref, mask_here))):
         copy = pltpu.make_async_copy(src, dst, in_sem.at[at])
         copy.start()
         small.append(copy)
-    loaded = pltpu.make_async_copy(x_ref, x_here, in_sem.at[3])
-    loaded.start()
     for copy in small:
         copy.wait()
     spectra(

time: 29.7 us -> 29.7 us (level)
  no operation moved by 1% of the time
where the time goes in v7:
time: 29.7 us; the launch traced here: 29.6 us
  Pallas kernels  29.6 us (100%)
    pallas_call x1, Pallas kernels, gather(): pl.pallas_call(gather_kernel, out_shape=(jax.ShapeDtypeStruct((32, WIDE),...  23.7 us
    pallas_call x1, Pallas kernels, correlate(): pl.pallas_call(correlate_kernel, out_shape=jax.ShapeDtypeStruct((60, 2, 3...  5.91 us

profile of v7, /device:TPU:1, one launch (start us, length us, event | category | flops | bytes accessed | tf_op | source)
XLA Modules:
  0.0 29.6 jit_solution(10390289020652353044)
XLA Ops:
  0.0 23.7 %gather.1 = (bf16[32,1280]{1,0:T(8,128)(2,1)S(1)}, bf16[4,4,2,32,1280]{4,3,2,1,0:T(8,128)(2,1)S(1)}) custom-call(bf16[1,8,150000]{2,1,0:T(8,128)(2,1)} %x_ref.1, bf16[1,20]{1,0:T(2,128)(2,1)} %bitcast.5, s32[1,240]{1,0:T(1,128)} %bitcast.4, s32[1,8]{1,0:T(1,128)} %mask_ref.1), custom_call_target="tpu_custom_call" | custom-call | tf_op jit(solution)/shard_map/gather/pallas_call | solution.py:368
  23.7 5.9 %correlate.1 = f32[60,2,32,1024]{3,2,1,0:T(8,128)} custom-call(bf16[32,1280]{1,0:T(8,128)(2,1)S(1)} %get-tuple-element.7.own_ref, bf16[32,32,1280]{2,1,0:T(8,128)(2,1)S(1)} %bitcast.3), custom_call_target="tpu_custom_call" | custom-call | tf_op jit(solution)/shard_map/correlate/pallas_call | solution.py:442
